TPU v7x, 256 devices: a whole 4x4x8 slice. The times are simulated.
256 devices in a mesh: outer: 8 (over y, x_lo), inner: 32 (over z, x_hi, core).
Axes of the slice: x: 4 (x_hi: 2, x_lo: 2; x = x_hi * 2 + x_lo), y: 4, z: 8, core: 2. Of those that a mesh axis runs over, the one named last changes fastest.
Arguments:
- queries: bfloat16 [65536, 4096], P(('outer', 'inner')), may hold values from -6 to 6
- keys: bfloat16 [65536, 1024], P(('outer', 'inner')), may hold values from -6 to 6
- values: bfloat16 [65536, 1024], P(('outer', 'inner')), may hold values from -6 to 6
- grad_out: bfloat16 [65536, 4096], P(('outer', 'inner')), may hold values from -24 to 24
- log_sum: float32 [32, 65536], P(None, ('outer', 'inner')), as said below
- row_delta: float32 [32, 65536], P(None, ('outer', 'inner')), may hold values from -24 to 24
- piece_index: int32 [512], P(('outer', 'inner')), may hold values from 0 to 511, as said below
Outputs:
- grad_queries: bfloat16 [65536, 4096], P(('outer', 'inner'))
- grad_keys: float32 [65536, 1024], P(('outer', 'inner'))
- grad_values: float32 [65536, 1024], P(('outer', 'inner'))
Inputs may be any that keep to these rules, and one draw needn't show every extreme that they name: `piece_index`: block b holds pieces p and 511 - p, the smaller first, where p runs over a permutation of 0 to 255 drawn from the seed; every piece appears once. `log_sum`: every entry lies within 1.5 of log(512).
All inputs are finite; a program needn't handle non-finite values.
Results may differ from a plain program's by a relative error of at most 0.0075.
Values may be sent and summed in bfloat16 or wider, within the bound.
A program may use at most 192 MiB of HBM per device.

v0:
```python
import functools
import math

import jax
import jax.numpy as jnp
from jax import lax
from jax.experimental import pallas as pl
from jax.experimental.pallas import tpu as pltpu
from jax.sharding import PartitionSpec as P

HEAD_DIM = 128
HALF = 128
MESH = pl.DeviceIdType.MESH
SCALE = 1.0 / math.sqrt(HEAD_DIM)
LOG2E = math.log2(math.e)
COMM = True
COMPUTE = True

BF16 = jnp.bfloat16
F32 = jnp.float32


def dot_nt(a, b):
    return lax.dot_general(a, b, (((1,), (1,)), ((), ())), preferred_element_type=F32)


def dot_nn(a, b):
    return lax.dot_general(a, b, (((1,), (0,)), ((), ())), preferred_element_type=F32)


def quadrant(k, v, q, do, lse2, delta, keep=None):
    p = jnp.exp2(dot_nt(k, q) * (SCALE * LOG2E) - lse2)
    if keep is not None:
        p = jnp.where(keep, p, 0.0)
    ds = p * (dot_nt(v, do) - delta)
    return p.astype(BF16), ds.astype(BF16)


def kernel(
    group,
    n_outer,
    n_inner,
    q_hbm,
    k_hbm,
    v_hbm,
    do_hbm,
    lse_hbm,
    delta_hbm,
    piece_ref,
    gq_hbm,
    gk_hbm,
    gv_hbm,
    q_v,
    do_v,
    lse_v,
    delta_v,
    lse_c,
    delta_c,
    kv_own,
    kv_grp,
    kv_far,
    kv_near,
    gq_acc,
    gq_out,
    own32,
    far32,
    grp32,
    n_send,
    n_recv,
    f_send,
    f_recv,
    s_send,
    s_recv,
    tile,
    flag,
    in_sem,
    out_sem,
    tile_sem,
    send_sem,
    recv_sem,
):
    chunks = kv_own.shape[0]
    o = lax.axis_index("outer")
    i = lax.axis_index("inner")
    core = lax.rem(i, 2)
    o_next, o_prev = lax.rem(o + 1, n_outer), lax.rem(o + n_outer - 1, n_outer)
    i_far, i_back = lax.rem(i + 2, n_inner), lax.rem(i + n_inner - 2, n_inner)
    to_next = (o_next, i)
    to_prev = (o_prev, i)
    to_far = (o_prev, i_far)
    to_back = (o_next, i_back)
    partner = (o, i + 1 - 2 * core)

    def remote(src, dst, kind, g, device):
        return pltpu.make_async_remote_copy(
            src_ref=src,
            dst_ref=dst,
            send_sem=send_sem.at[kind, g],
            recv_sem=recv_sem.at[kind, g],
            device_id=device,
            device_id_type=MESH,
        )

    def hop_group(g):
        return remote(kv_own.at[g], kv_grp.at[g], 0, g, to_next)

    def hop_far(g):
        return remote(kv_grp.at[g], kv_far.at[g], 1, g, to_far)

    def hop_near_own(g):
        return remote(kv_own.at[g], kv_near.at[g], 2, g, partner)

    def hop_near_far(g):
        return remote(kv_far.at[g], kv_near.at[g], 2, g, partner)

    def back_near(g):
        return remote(n_send.at[g], n_recv.at[g], 3, g, partner)

    def back_far(g):
        return remote(f_send.at[g], f_recv.at[g], 4, g, to_back)

    def back_sum(g):
        return remote(s_send.at[g], s_recv.at[g], 5, g, to_prev)

    def tile_copy(src, dst, kind, device):
        return pltpu.make_async_remote_copy(
            src_ref=tile.at[src],
            dst_ref=tile.at[dst],
            send_sem=tile_sem.at[0, kind],
            recv_sem=tile_sem.at[1, kind],
            device_id=device,
            device_id_type=MESH,
        )

    def load_kv(g):
        cols = pl.ds(g * HEAD_DIM, HEAD_DIM)
        return (
            pltpu.make_async_copy(k_hbm.at[:, cols], kv_own.at[g, 0], in_sem.at[0, g]),
            pltpu.make_async_copy(v_hbm.at[:, cols], kv_own.at[g, 1], in_sem.at[1, g]),
        )

    def load_q(g):
        cols = pl.ds(g * group * HEAD_DIM, group * HEAD_DIM)
        return (
            pltpu.make_async_copy(q_hbm.at[:, cols], q_v.at[g], in_sem.at[2, g]),
            pltpu.make_async_copy(do_hbm.at[:, cols], do_v.at[g], in_sem.at[3, g]),
        )

    def load_rows():
        return (
            pltpu.make_async_copy(lse_hbm, lse_v, in_sem.at[4, 0]),
            pltpu.make_async_copy(delta_hbm, delta_v, in_sem.at[4, 1]),
        )

    def store_q(g):
        cols = pl.ds(g * group * HEAD_DIM, group * HEAD_DIM)
        return pltpu.make_async_copy(gq_out.at[g], gq_hbm.at[:, cols], out_sem.at[0, g])

    def store_kv(g):
        cols = pl.ds(g * HEAD_DIM, HEAD_DIM)
        return (
            pltpu.make_async_copy(own32.at[g, 0], gk_hbm.at[:, cols], out_sem.at[1, g]),
            pltpu.make_async_copy(own32.at[g, 1], gv_hbm.at[:, cols], out_sem.at[2, g]),
        )

    for g in range(chunks):
        for copy in load_kv(g):
            copy.start()
    for copy in load_rows():
        copy.start()
    for g in range(chunks):
        for copy in load_q(g):
            copy.start()

    tile[0] = jnp.full(tile.shape[1:], piece_ref[0].astype(F32), F32)

    if COMM:
        barrier = pltpu.get_barrier_semaphore()
        for peer in (to_next, to_prev, to_far, to_back, partner):
            pl.semaphore_signal(barrier, inc=1, device_id=peer, device_id_type=MESH)
        pl.semaphore_wait(barrier, 5)
        tile_copy(0, 1, 0, to_next).start()

        @pl.when(core == 0)
        def _():
            tile_copy(0, 3, 2, partner).start()

    def send_own(g, carry):
        for copy in load_kv(g):
            copy.wait()
        if COMM:
            hop_group(g).start()

            @pl.when(core == 0)
            def _():
                hop_near_own(g).start()

        return carry

    lax.fori_loop(0, chunks, send_own, 0)
    for copy in load_rows():
        copy.wait()
    for g in range(chunks):
        lse_c[g] = lse_v[g * group : (g + 1) * group] * LOG2E
        delta_c[g] = delta_v[g * group : (g + 1) * group]

    def rows_of(ref, g, j, half):
        return ref[g, j : j + 1, half * HALF : (half + 1) * HALF]

    def head(ref, g, j, half):
        return ref[g, pl.ds(half * HALF, HALF), pl.ds(j * HEAD_DIM, HEAD_DIM)]

    def over_heads(parts):
        return jnp.concatenate(parts, axis=1)

    def own(g):
        keep = lax.broadcasted_iota(jnp.int32, (HALF, HALF), 0) <= lax.broadcasted_iota(
            jnp.int32, (HALF, HALF), 1
        )
        k0, k1 = kv_own[g, 0, :HALF], kv_own[g, 0, HALF:]
        v0, v1 = kv_own[g, 1, :HALF], kv_own[g, 1, HALF:]
        p_0, s_0, p_1, s_1 = [], [], [], []
        q_all, do_all = [], []
        for j in range(group):
            lse0 = rows_of(lse_c, g, j, 0)
            lse1 = rows_of(lse_c, g, j, 1)
            delta0 = rows_of(delta_c, g, j, 0)
            delta1 = rows_of(delta_c, g, j, 1)
            q0, q1 = head(q_v, g, j, 0), head(q_v, g, j, 1)
            do0, do1 = head(do_v, g, j, 0), head(do_v, g, j, 1)
            p00, s00 = quadrant(k0, v0, q0, do0, lse0, delta0, keep)
            p01, s01 = quadrant(k0, v0, q1, do1, lse1, delta1)
            p11, s11 = quadrant(k1, v1, q1, do1, lse1, delta1, keep)
            cols = pl.ds(j * HEAD_DIM, HEAD_DIM)
            gq_acc[g, :HALF, cols] = dot_nn(s00.T, k0)
            gq_acc[g, HALF:, cols] = dot_nn(
                jnp.concatenate([s01, s11], axis=0).T, kv_own[g, 0]
            )
            p_0 += [p00, p01]
            s_0 += [s00, s01]
            p_1.append(p11)
            s_1.append(s11)
            q_all += [q0, q1]
            do_all += [do0, do1]
        q_both = jnp.concatenate(q_all, axis=0)
        do_both = jnp.concatenate(do_all, axis=0)
        q_late = jnp.concatenate(q_all[1::2], axis=0)
        do_late = jnp.concatenate(do_all[1::2], axis=0)
        own32[g, 0, :HALF] = dot_nn(over_heads(s_0), q_both)
        own32[g, 0, HALF:] = dot_nn(over_heads(s_1), q_late)
        own32[g, 1, :HALF] = dot_nn(over_heads(p_0), do_both)
        own32[g, 1, HALF:] = dot_nn(over_heads(p_1), do_late)

    def other(g, kv_ref, which, out, as_type, last):
        early = flag[which] == 1
        k0, k1 = kv_ref[g, 0, :HALF], kv_ref[g, 0, HALF:]
        v0, v1 = kv_ref[g, 1, :HALF], kv_ref[g, 1, HALF:]
        kb, vb = jnp.where(early, k0, k1), jnp.where(early, v0, v1)
        p_a, s_a, p_b, s_b = [], [], [], []
        q_a, do_a, q_b, do_b = [], [], [], []
        for j in range(group):
            lse1 = rows_of(lse_c, g, j, 1)
            lseb = jnp.where(early, rows_of(lse_c, g, j, 0), lse1)
            delta1 = rows_of(delta_c, g, j, 1)
            deltab = jnp.where(early, rows_of(delta_c, g, j, 0), delta1)
            q1, do1 = head(q_v, g, j, 1), head(do_v, g, j, 1)
            qb = jnp.where(early, head(q_v, g, j, 0), q1)
            dob = jnp.where(early, head(do_v, g, j, 0), do1)
            pa, sa = quadrant(k0, v0, q1, do1, lse1, delta1)
            pb, sb = quadrant(kb, vb, qb, dob, lseb, deltab)
            gq_a, gq_b = dot_nn(sa.T, k0), dot_nn(sb.T, kb)
            cols = pl.ds(j * HEAD_DIM, HEAD_DIM)
            zero = jnp.zeros_like(gq_b)
            new0 = gq_acc[g, :HALF, cols] + jnp.where(early, gq_b, zero)
            new1 = gq_acc[g, HALF:, cols] + (gq_a + jnp.where(early, zero, gq_b))
            if last:
                gq_out[g, :HALF, cols] = (new0 * SCALE).astype(BF16)
                gq_out[g, HALF:, cols] = (new1 * SCALE).astype(BF16)
            else:
                gq_acc[g, :HALF, cols] = new0
                gq_acc[g, HALF:, cols] = new1
            p_a.append(pa)
            s_a.append(sa)
            p_b.append(pb)
            s_b.append(sb)
            q_a.append(q1)
            do_a.append(do1)
            q_b.append(qb)
            do_b.append(dob)
        for t, (xa, ya, xb, yb) in enumerate(((s_a, q_a, s_b, q_b), (p_a, do_a, p_b, do_b))):
            first = dot_nn(over_heads(xa), jnp.concatenate(ya, axis=0))
            second = dot_nn(over_heads(xb), jnp.concatenate(yb, axis=0))
            zero = jnp.zeros_like(second)
            out[g, t, :HALF] = (first + jnp.where(early, second, zero)).astype(as_type)
            out[g, t, HALF:] = jnp.where(early, zero, second).astype(as_type)

    def set_flag(which):
        mine = jnp.max(tile[0])
        flag[which] = (jnp.max(tile[which]) < mine).astype(jnp.int32)

    def step(t, carry):
        @pl.when(t < chunks)
        def _():
            g = t
            for copy in load_q(g):
                copy.wait()
            if COMPUTE:
                own(g)
            if COMM:
                hop_group(g).wait_recv()
                hop_far(g).start()

        if COMM:

            @pl.when(t == 0)
            def _():
                tile_copy(0, 1, 0, to_next).wait_recv()
                tile_copy(1, 2, 1, to_far).start()
                set_flag(1)

            @pl.when(t == 1)
            def _():
                tile_copy(1, 2, 1, to_far).wait_recv()

                @pl.when(core == 1)
                def _():
                    tile_copy(2, 3, 2, partner).start()

                set_flag(2)
                tile_copy(2, 3, 2, partner).wait_recv()
                set_flag(3)

        @pl.when((t >= 1) & (t < chunks + 1))
        def _():
            g = t - 1
            if COMM:
                hop_far(g).wait_recv()

                @pl.when(core == 1)
                def _():
                    hop_near_far(g).start()

                hop_near_own(g).wait_recv()
            if COMPUTE:
                other(g, kv_near, 3, n_send, BF16, False)
            if COMM:
                back_near(g).start()
            if COMPUTE:
                other(g, kv_far, 2, far32, F32, False)
                other(g, kv_grp, 1, grp32, F32, True)
            store_q(g).start()

        @pl.when((t >= 2) & (t < chunks + 2))
        def _():
            g = t - 2

            @pl.when(core == 0)
            def _():
                f_send[g] = far32[g].astype(BF16)

            @pl.when(core == 1)
            def _():
                if COMM:
                    back_near(g).wait_recv()
                f_send[g] = (far32[g] + n_recv[g].astype(F32)).astype(BF16)

            if COMM:
                back_far(g).start()

        @pl.when((t >= 3) & (t < chunks + 3))
        def _():
            g = t - 3
            if COMM:
                back_far(g).wait_recv()
            s_send[g] = (grp32[g] + f_recv[g].astype(F32)).astype(BF16)
            if COMM:
                back_sum(g).start()

        @pl.when((t >= 4) & (t < chunks + 4))
        def _():
            g = t - 4
            if COMM:
                back_sum(g).wait_recv()
            total = own32[g] + s_recv[g].astype(F32)

            @pl.when(core == 0)
            def _():
                if COMM:
                    back_near(g).wait_recv()
                both = total + n_recv[g].astype(F32)
                own32[g, 0] = both[0] * SCALE
                own32[g, 1] = both[1]

            @pl.when(core == 1)
            def _():
                own32[g, 0] = total[0] * SCALE
                own32[g, 1] = total[1]

            for copy in store_kv(g):
                copy.start()

        return carry

    lax.fori_loop(0, chunks + 4, step, 0)

    def drain(g, carry):
        store_q(g).wait()
        for copy in store_kv(g):
            copy.wait()
        if COMM:
            hop_group(g).wait_send()
            hop_far(g).wait_send()
            hop_near_own(g).wait_send()
            back_near(g).wait_send()
            back_far(g).wait_send()
            back_sum(g).wait_send()
        return carry

    lax.fori_loop(0, chunks, drain, 0)
    if COMM:
        tile_copy(0, 1, 0, to_next).wait_send()
        tile_copy(1, 2, 1, to_far).wait_send()
        tile_copy(0, 3, 2, partner).wait_send()


def on_device(n_outer, n_inner, queries, keys, values, grad_out, log_sum, row_delta, piece_index):
    rows = queries.shape[0]
    chunks = keys.shape[1] // HEAD_DIM
    group = queries.shape[1] // keys.shape[1]
    wide = (chunks, rows, group * HEAD_DIM)
    pair = (chunks, 2, rows, HEAD_DIM)
    hbm = pl.BlockSpec(memory_space=pl.ANY)
    vmem = pltpu.VMEM
    return pl.pallas_call(
        functools.partial(kernel, group, n_outer, n_inner),
        out_shape=(
            jax.ShapeDtypeStruct(queries.shape, BF16),
            jax.ShapeDtypeStruct(keys.shape, F32),
            jax.ShapeDtypeStruct(values.shape, F32),
        ),
        in_specs=[hbm] * 6 + [pl.BlockSpec(memory_space=pltpu.SMEM)],
        out_specs=(hbm, hbm, hbm),
        scratch_shapes=[
            vmem(wide, BF16),
            vmem(wide, BF16),
            vmem(log_sum.shape, F32),
            vmem(row_delta.shape, F32),
            vmem((chunks, group, rows), F32),
            vmem((chunks, group, rows), F32),
            vmem(pair, BF16),
            vmem(pair, BF16),
            vmem(pair, BF16),
            vmem(pair, BF16),
            vmem(wide, F32),
            vmem(wide, BF16),
            vmem(pair, F32),
            vmem(pair, F32),
            vmem(pair, F32),
            vmem(pair, BF16),
            vmem(pair, BF16),
            vmem(pair, BF16),
            vmem(pair, BF16),
            vmem(pair, BF16),
            vmem(pair, BF16),
            vmem((4, 8, 128), F32),
            pltpu.SMEM((4,), jnp.int32),
            pltpu.SemaphoreType.DMA((5, chunks)),
            pltpu.SemaphoreType.DMA((3, chunks)),
            pltpu.SemaphoreType.DMA((2, 3)),
            pltpu.SemaphoreType.DMA((6, chunks)),
            pltpu.SemaphoreType.DMA((6, chunks)),
        ],
        compiler_params=pltpu.CompilerParams(
            collective_id=0 if COMM else None, has_side_effects=True, vmem_limit_bytes=48 * 1024 * 1024
        ),
        cost_estimate=pl.CostEstimate(
            flops=6_000_000_000, bytes_accessed=10_000_000, transcendentals=5_000_000
        ),
    )(queries, keys, values, grad_out, log_sum, row_delta, piece_index)


def solution(mesh):
    in_specs = (
        P(("outer", "inner"), None),
        P(("outer", "inner"), None),
        P(("outer", "inner"), None),
        P(("outer", "inner"), None),
        P(None, ("outer", "inner")),
        P(None, ("outer", "inner")),
        P(("outer", "inner")),
    )
    out_specs = (
        P(("outer", "inner"), None),
        P(("outer", "inner"), None),
        P(("outer", "inner"), None),
    )
    body = functools.partial(on_device, mesh.shape["outer"], mesh.shape["inner"])
    return jax.shard_map(
        body, mesh=mesh, in_specs=in_specs, out_specs=out_specs, check_vma=False
    )
```

profile of v0, /device:TPU:26, one launch (start us, length us, event | category | flops | bytes accessed | tf_op | source)
XLA Modules:
  0.0 97.2 jit_solution(5525539939004263754)
XLA Ops:
  0.6 0.0 copy-start
  0.6 1.0 %copy-done = bf16[256,1024]{1,0:T(8,128)(2,1)S(1)} copy-done((bf16[256,1024]{1,0:T(8,128)(2,1)S(1)}, bf16[256,1024]{1,0:T(8,128)(2,1)}, u32[]{:S(2)}) %copy-start) | copy-done | bytes 524312
  1.7 0.0 copy-start.1
  1.7 1.0 %copy-done.1 = bf16[256,1024]{1,0:T(8,128)(2,1)S(1)} copy-done((bf16[256,1024]{1,0:T(8,128)(2,1)S(1)}, bf16[256,1024]{1,0:T(8,128)(2,1)}, u32[]{:S(2)}) %copy-start.1) | copy-done | bytes 524312
  2.7 0.0 copy-start.2
  2.7 0.8 copy-done.2
  3.5 0.0 copy-start.3
  3.5 0.8 copy-done.3
  4.2 0.0 copy-start.4
  4.2 0.7 copy-done.4
  4.9 89.1 %shard_map.94 = (bf16[256,4096]{1,0:T(8,128)(2,1)S(1)}, f32[256,1024]{1,0:T(8,128)S(1)}, f32[256,1024]{1,0:T(8,128)S(1)}) custom-call(bf16[256,4096]{1,0:T(8,128)(2,1)} %q_hbm.1, bf16[256,1024]{1,0:T(8,128)(2,1)S(1)} %copy-done, bf16[256,1024]{1,0:T(8,128)(2,1)S(1)} %copy-done.1, bf16[256,4096]{1,0:T(8,128)(2,1)} %do_hbm.1, f32[32,256]{1,0:T(8,128)S(1)} %copy-done.2, ...), custom_call_target="tpu_custom_call" | custom-call | flops 6000000000 | bytes 10000000 | tf_op jit(solution)/shard_map/pallas_call | solution.py:434
  94.0 1.3 %copy.13 = bf16[256,4096]{1,0:T(8,128)(2,1)} copy(bf16[256,4096]{1,0:T(8,128)(2,1)S(1)} %get-tuple-element.6) | data formatting | bytes 4194304
  95.3 1.0 copy.14
  96.3 1.0 copy.15
Async XLA Ops:
  0.6 1.0 %copy-start = (bf16[256,1024]{1,0:T(8,128)(2,1)S(1)}, bf16[256,1024]{1,0:T(8,128)(2,1)}, u32[]{:S(2)}) copy-start(bf16[256,1024]{1,0:T(8,128)(2,1)} %k_hbm.1) | copy-start | bytes 1572868
  1.7 1.0 %copy-start.1 = (bf16[256,1024]{1,0:T(8,128)(2,1)S(1)}, bf16[256,1024]{1,0:T(8,128)(2,1)}, u32[]{:S(2)}) copy-start(bf16[256,1024]{1,0:T(8,128)(2,1)} %v_hbm.1) | copy-start | bytes 1572868
  2.7 0.8 copy-start.2
  3.5 0.8 copy-start.3
  4.2 0.7 copy-start.4
where the time goes:
time: 97.6 us; the launch traced here: 97.2 us
  Pallas kernels  89.1 us (91%)
  local copies, waits for them, and re-layouts  7.51 us (8%)
    pallas_call x1, Pallas kernels, on_device(): pl.pallas_call(functools.partial(kernel, group, n_outer, n_inner), out_sh...  89.1 us
    unnamed x13, local copies, waits for them, and re-layouts  7.51 us

commit v1 on v0

--- a/solution.py
+++ b/solution.py
@@ -14,6 +14,7 @@
 SCALE = 1.0 / math.sqrt(HEAD_DIM)
 LOG2E = math.log2(math.e)
 COMM = True
+LEAD = 4
 COMPUTE = True
 
 BF16 = jnp.bfloat16
@@ -50,6 +51,8 @@
     gq_hbm,
     gk_hbm,
     gv_hbm,
+    k_v,
+    v_v,
     q_v,
     do_v,
     lse_v,
@@ -57,18 +60,19 @@
     lse_c,
     delta_c,
     kv_own,
-    kv_grp,
+    kv_hop,
     kv_far,
     kv_near,
+    gq_own,
     gq_acc,
     gq_out,
     own32,
-    far32,
-    grp32,
     n_send,
     n_recv,
     f_send,
     f_recv,
+    g_send,
+    g_recv,
     s_send,
     s_recv,
     tile,
@@ -83,13 +87,16 @@
     o = lax.axis_index("outer")
     i = lax.axis_index("inner")
     core = lax.rem(i, 2)
-    o_next, o_prev = lax.rem(o + 1, n_outer), lax.rem(o + n_outer - 1, n_outer)
+    odd = lax.rem(o, 2)
+    o_pair = o + 1 - 2 * odd
     i_far, i_back = lax.rem(i + 2, n_inner), lax.rem(i + n_inner - 2, n_inner)
-    to_next = (o_next, i)
-    to_prev = (o_prev, i)
-    to_far = (o_prev, i_far)
-    to_back = (o_next, i_back)
+    to_pair = (o_pair, i)
+    to_far = (o_pair, i_far)
+    to_back = (o_pair, i_back)
+    to_up = (lax.rem(o + 2, n_outer), i)
+    to_down = (lax.rem(o + n_outer - 2, n_outer), i)
     partner = (o, i + 1 - 2 * core)
+    kv_grp = kv_hop.at[0]
 
     def remote(src, dst, kind, g, device):
         return pltpu.make_async_remote_copy(
@@ -101,11 +108,14 @@
             device_id_type=MESH,
         )
 
-    def hop_group(g):
-        return remote(kv_own.at[g], kv_grp.at[g], 0, g, to_next)
+    def hop_pair(g):
+        return remote(kv_own.at[g], kv_hop.at[odd, g], 0, g, to_pair)
 
     def hop_far(g):
-        return remote(kv_grp.at[g], kv_far.at[g], 1, g, to_far)
+        return remote(kv_hop.at[1 - odd, g], kv_far.at[g], 1, g, to_far)
+
+    def hop_up(g):
+        return remote(kv_hop.at[1, g], kv_hop.at[0, g], 6, g, to_up)
 
     def hop_near_own(g):
         return remote(kv_own.at[g], kv_near.at[g], 2, g, partner)
@@ -120,7 +130,10 @@
         return remote(f_send.at[g], f_recv.at[g], 4, g, to_back)
 
     def back_sum(g):
-        return remote(s_send.at[g], s_recv.at[g], 5, g, to_prev)
+        return remote(s_send.at[g], s_recv.at[g], 5, g, to_pair)
+
+    def back_down(g):
+        return remote(g_send.at[g], g_recv.at[g], 7, g, to_down)
 
     def tile_copy(src, dst, kind, device):
         return pltpu.make_async_remote_copy(
@@ -132,11 +145,22 @@
             device_id_type=MESH,
         )
 
-    def load_kv(g):
-        cols = pl.ds(g * HEAD_DIM, HEAD_DIM)
+    def tile_pair():
+        return tile_copy(0, 1 + 3 * odd, 0, to_pair)
+
+    def tile_far():
+        return tile_copy(4 - 3 * odd, 2, 1, to_far)
+
+    def tile_near():
+        return tile_copy(2 * core, 3, 2, partner)
+
+    def tile_up():
+        return tile_copy(4, 1, 3, to_up)
+
+    def load_kv():
         return (
-            pltpu.make_async_copy(k_hbm.at[:, cols], kv_own.at[g, 0], in_sem.at[0, g]),
-            pltpu.make_async_copy(v_hbm.at[:, cols], kv_own.at[g, 1], in_sem.at[1, g]),
+            pltpu.make_async_copy(k_hbm, k_v, in_sem.at[0, 0]),
+            pltpu.make_async_copy(v_hbm, v_v, in_sem.at[1, 0]),
         )
 
     def load_q(g):
@@ -163,9 +187,8 @@
             pltpu.make_async_copy(own32.at[g, 1], gv_hbm.at[:, cols], out_sem.at[2, g]),
         )
 
-    for g in range(chunks):
-        for copy in load_kv(g):
-            copy.start()
+    for copy in load_kv():
+        copy.start()
     for copy in load_rows():
         copy.start()
     for g in range(chunks):
@@ -176,20 +199,28 @@
 
     if COMM:
         barrier = pltpu.get_barrier_semaphore()
-        for peer in (to_next, to_prev, to_far, to_back, partner):
+        for peer in (to_pair, to_far, to_back, partner):
             pl.semaphore_signal(barrier, inc=1, device_id=peer, device_id_type=MESH)
-        pl.semaphore_wait(barrier, 5)
-        tile_copy(0, 1, 0, to_next).start()
+
+        @pl.when(odd == 0)
+        def _():
+            for peer in (to_up, to_down):
+                pl.semaphore_signal(barrier, inc=1, device_id=peer, device_id_type=MESH)
+            pl.semaphore_wait(barrier, 6)
+
+        @pl.when(odd == 1)
+        def _():
+            pl.semaphore_wait(barrier, 4)
+
+        tile_pair().start()
 
         @pl.when(core == 0)
         def _():
-            tile_copy(0, 3, 2, partner).start()
+            tile_near().start()
 
     def send_own(g, carry):
-        for copy in load_kv(g):
-            copy.wait()
         if COMM:
-            hop_group(g).start()
+            hop_pair(g).start()
 
             @pl.when(core == 0)
             def _():
@@ -197,8 +228,13 @@
 
         return carry
 
-    lax.fori_loop(0, chunks, send_own, 0)
-    for copy in load_rows():
+    for copy in load_kv():
+        copy.wait()
+    for g in range(chunks):
+        kv_own[g, 0] = k_v[:, g * HEAD_DIM : (g + 1) * HEAD_DIM]
+        kv_own[g, 1] = v_v[:, g * HEAD_DIM : (g + 1) * HEAD_DIM]
+    lax.fori_loop(0, LEAD, send_own, 0)
+    for copy in load_rows() + load_q(0):
         copy.wait()
     for g in range(chunks):
         lse_c[g] = lse_v[g * group : (g + 1) * group] * LOG2E
@@ -231,17 +267,20 @@
             p00, s00 = quadrant(k0, v0, q0, do0, lse0, delta0, keep)
             p01, s01 = quadrant(k0, v0, q1, do1, lse1, delta1)
             p11, s11 = quadrant(k1, v1, q1, do1, lse1, delta1, keep)
-            cols = pl.ds(j * HEAD_DIM, HEAD_DIM)
-            gq_acc[g, :HALF, cols] = dot_nn(s00.T, k0)
-            gq_acc[g, HALF:, cols] = dot_nn(
-                jnp.concatenate([s01, s11], axis=0).T, kv_own[g, 0]
-            )
             p_0 += [p00, p01]
             s_0 += [s00, s01]
             p_1.append(p11)
             s_1.append(s11)
             q_all += [q0, q1]
             do_all += [do0, do1]
+        early = dot_nn(over_heads(s_0[0::2]).T, k0)
+        late = dot_nn(
+            jnp.concatenate([over_heads(s_0[1::2]).T, over_heads(s_1).T], axis=1), kv_own[g, 0]
+        )
+        for j in range(group):
+            cols = pl.ds(j * HEAD_DIM, HEAD_DIM)
+            gq_own[g, :HALF, cols] = early[j * HALF : (j + 1) * HALF]
+            gq_own[g, HALF:, cols] = late[j * HALF : (j + 1) * HALF]
         q_both = jnp.concatenate(q_all, axis=0)
         do_both = jnp.concatenate(do_all, axis=0)
         q_late = jnp.concatenate(q_all[1::2], axis=0)
@@ -251,7 +290,7 @@
         own32[g, 1, :HALF] = dot_nn(over_heads(p_0), do_both)
         own32[g, 1, HALF:] = dot_nn(over_heads(p_1), do_late)
 
-    def other(g, kv_ref, which, out, as_type, last):
+    def other(g, kv_ref, which, out, first):
         early = flag[which] == 1
         k0, k1 = kv_ref[g, 0, :HALF], kv_ref[g, 0, HALF:]
         v0, v1 = kv_ref[g, 1, :HALF], kv_ref[g, 1, HALF:]
@@ -268,17 +307,6 @@
             dob = jnp.where(early, head(do_v, g, j, 0), do1)
             pa, sa = quadrant(k0, v0, q1, do1, lse1, delta1)
             pb, sb = quadrant(kb, vb, qb, dob, lseb, deltab)
-            gq_a, gq_b = dot_nn(sa.T, k0), dot_nn(sb.T, kb)
-            cols = pl.ds(j * HEAD_DIM, HEAD_DIM)
-            zero = jnp.zeros_like(gq_b)
-            new0 = gq_acc[g, :HALF, cols] + jnp.where(early, gq_b, zero)
-            new1 = gq_acc[g, HALF:, cols] + (gq_a + jnp.where(early, zero, gq_b))
-            if last:
-                gq_out[g, :HALF, cols] = (new0 * SCALE).astype(BF16)
-                gq_out[g, HALF:, cols] = (new1 * SCALE).astype(BF16)
-            else:
-                gq_acc[g, :HALF, cols] = new0
-                gq_acc[g, HALF:, cols] = new1
             p_a.append(pa)
             s_a.append(sa)
             p_b.append(pb)
@@ -287,52 +315,81 @@
             do_a.append(do1)
             q_b.append(qb)
             do_b.append(dob)
+        blank = jnp.zeros_like(k0)
+        weights = jnp.concatenate(
+            [jnp.concatenate([k0, blank], axis=1), jnp.concatenate([blank, kb], axis=1)], axis=0
+        )
+        both = dot_nn(jnp.concatenate([over_heads(s_a).T, over_heads(s_b).T], axis=1), weights)
+        for j in range(group):
+            cols = pl.ds(j * HEAD_DIM, HEAD_DIM)
+            gq_a = both[j * HALF : (j + 1) * HALF, :HEAD_DIM]
+            gq_b = both[j * HALF : (j + 1) * HALF, HEAD_DIM:]
+            zero = jnp.zeros_like(gq_b)
+            add0 = jnp.where(early, gq_b, zero)
+            add1 = gq_a + jnp.where(early, zero, gq_b)
+            if first:
+                gq_acc[g, :HALF, cols] = add0
+                gq_acc[g, HALF:, cols] = add1
+            else:
+                gq_acc[g, :HALF, cols] += add0
+                gq_acc[g, HALF:, cols] += add1
         for t, (xa, ya, xb, yb) in enumerate(((s_a, q_a, s_b, q_b), (p_a, do_a, p_b, do_b))):
-            first = dot_nn(over_heads(xa), jnp.concatenate(ya, axis=0))
+            one = dot_nn(over_heads(xa), jnp.concatenate(ya, axis=0))
             second = dot_nn(over_heads(xb), jnp.concatenate(yb, axis=0))
             zero = jnp.zeros_like(second)
-            out[g, t, :HALF] = (first + jnp.where(early, second, zero)).astype(as_type)
-            out[g, t, HALF:] = jnp.where(early, zero, second).astype(as_type)
+            out[g, t, :HALF] = (one + jnp.where(early, second, zero)).astype(BF16)
+            out[g, t, HALF:] = jnp.where(early, zero, second).astype(BF16)
 
     def set_flag(which):
         mine = jnp.max(tile[0])
         flag[which] = (jnp.max(tile[which]) < mine).astype(jnp.int32)
 
+    if COMPUTE:
+        own(0)
+    for g in range(1, chunks):
+        for copy in load_q(g):
+            copy.wait()
+
     def step(t, carry):
         @pl.when(t < chunks)
         def _():
             g = t
-            for copy in load_q(g):
-                copy.wait()
-            if COMPUTE:
-                own(g)
-            if COMM:
-                hop_group(g).wait_recv()
+            if COMM:
+                hop_pair(g).wait_recv()
                 hop_far(g).start()
 
+            @pl.when(g + LEAD < chunks)
+            def _():
+                send_own(g + LEAD, 0)
+
+            if COMM:
+
+                @pl.when(odd == 0)
+                def _():
+                    hop_up(g).start()
+
         if COMM:
 
             @pl.when(t == 0)
             def _():
-                tile_copy(0, 1, 0, to_next).wait_recv()
-                tile_copy(1, 2, 1, to_far).start()
-                set_flag(1)
+                tile_pair().wait_recv()
+                tile_far().start()
+
+                @pl.when(odd == 0)
+                def _():
+                    tile_up().start()
 
             @pl.when(t == 1)
             def _():
-                tile_copy(1, 2, 1, to_far).wait_recv()
+                tile_far().wait_recv()
 
                 @pl.when(core == 1)
                 def _():
-                    tile_copy(2, 3, 2, partner).start()
-
-                set_flag(2)
-                tile_copy(2, 3, 2, partner).wait_recv()
-                set_flag(3)
-
-        @pl.when((t >= 1) & (t < chunks + 1))
-        def _():
-            g = t - 1
+                    tile_near().start()
+
+        @pl.when((t >= 2) & (t < chunks + 2))
+        def _():
+            g = t - 2
             if COMM:
                 hop_far(g).wait_recv()
 
@@ -340,45 +397,88 @@
                 def _():
                     hop_near_far(g).start()
 
+        if COMM:
+
+            @pl.when(t == 3)
+            def _():
+                @pl.when(odd == 0)
+                def _():
+                    tile_up().wait_recv()
+
+                tile_near().wait_recv()
+                for which in (1, 2, 3):
+                    set_flag(which)
+
+        @pl.when((t >= 3) & (t < chunks + 3))
+        def _():
+            g = t - 3
+            if COMM:
                 hop_near_own(g).wait_recv()
             if COMPUTE:
-                other(g, kv_near, 3, n_send, BF16, False)
+                other(g, kv_near, 3, n_send, True)
             if COMM:
                 back_near(g).start()
             if COMPUTE:
-                other(g, kv_far, 2, far32, F32, False)
-                other(g, kv_grp, 1, grp32, F32, True)
+                other(g, kv_far, 2, f_send, False)
+            if COMM:
+
+                @pl.when(core == 0)
+                def _():
+                    back_far(g).start()
+
+                @pl.when(odd == 0)
+                def _():
+                    hop_up(g).wait_recv()
+
+            if COMPUTE:
+                other(g, kv_grp, 1, g_send, False)
+            if COMM:
+
+                @pl.when(odd == 0)
+                def _():
+                    back_down(g).start()
+
+        if COMM:
+
+            @pl.when((t >= 4) & (t < chunks + 4) & (core == 1))
+            def _():
+                g = t - 4
+                back_near(g).wait_recv()
+                f_send[g] = (f_send[g].astype(F32) + n_recv[g].astype(F32)).astype(BF16)
+                back_far(g).start()
+
+        if COMPUTE:
+            @pl.when(t < 3)
+            def _():
+                own(t + 1)
+
+            @pl.when((t >= chunks + 3) & (t < 2 * chunks - 1))
+            def _():
+                own(t + 1 - chunks)
+
+        if COMM:
+
+            @pl.when((t >= 6) & (t < chunks + 6))
+            def _():
+                g = t - 6
+                back_far(g).wait_recv()
+
+                @pl.when(odd == 0)
+                def _():
+                    back_down(g).wait_recv()
+                    s_send[g] = (f_recv[g].astype(F32) + g_recv[g].astype(F32)).astype(BF16)
+
+                @pl.when(odd == 1)
+                def _():
+                    s_send[g] = (f_recv[g].astype(F32) + g_send[g].astype(F32)).astype(BF16)
+
+                back_sum(g).start()
+
+        @pl.when(t >= 8)
+        def _():
+            g = t - 8
+            gq_out[g] = ((gq_own[g] + gq_acc[g]) * SCALE).astype(BF16)
             store_q(g).start()
-
-        @pl.when((t >= 2) & (t < chunks + 2))
-        def _():
-            g = t - 2
-
-            @pl.when(core == 0)
-            def _():
-                f_send[g] = far32[g].astype(BF16)
-
-            @pl.when(core == 1)
-            def _():
-                if COMM:
-                    back_near(g).wait_recv()
-                f_send[g] = (far32[g] + n_recv[g].astype(F32)).astype(BF16)
-
-            if COMM:
-                back_far(g).start()
-
-        @pl.when((t >= 3) & (t < chunks + 3))
-        def _():
-            g = t - 3
-            if COMM:
-                back_far(g).wait_recv()
-            s_send[g] = (grp32[g] + f_recv[g].astype(F32)).astype(BF16)
-            if COMM:
-                back_sum(g).start()
-
-        @pl.when((t >= 4) & (t < chunks + 4))
-        def _():
-            g = t - 4
             if COMM:
                 back_sum(g).wait_recv()
             total = own32[g] + s_recv[g].astype(F32)
@@ -401,26 +501,36 @@
 
         return carry
 
-    lax.fori_loop(0, chunks + 4, step, 0)
+    lax.fori_loop(0, chunks + 8, step, 0)
 
     def drain(g, carry):
         store_q(g).wait()
         for copy in store_kv(g):
             copy.wait()
         if COMM:
-            hop_group(g).wait_send()
+            hop_pair(g).wait_send()
             hop_far(g).wait_send()
             hop_near_own(g).wait_send()
             back_near(g).wait_send()
             back_far(g).wait_send()
             back_sum(g).wait_send()
+
+            @pl.when(odd == 0)
+            def _():
+                hop_up(g).wait_send()
+                back_down(g).wait_send()
+
         return carry
 
     lax.fori_loop(0, chunks, drain, 0)
     if COMM:
-        tile_copy(0, 1, 0, to_next).wait_send()
-        tile_copy(1, 2, 1, to_far).wait_send()
-        tile_copy(0, 3, 2, partner).wait_send()
+        tile_pair().wait_send()
+        tile_far().wait_send()
+        tile_near().wait_send()
+
+        @pl.when(odd == 0)
+        def _():
+            tile_up().wait_send()
 
 
 def on_device(n_outer, n_inner, queries, keys, values, grad_out, log_sum, row_delta, piece_index):
@@ -429,7 +539,7 @@
     group = queries.shape[1] // keys.shape[1]
     wide = (chunks, rows, group * HEAD_DIM)
     pair = (chunks, 2, rows, HEAD_DIM)
-    hbm = pl.BlockSpec(memory_space=pl.ANY)
+    hbm = pl.BlockSpec(memory_space=pltpu.HBM)
     vmem = pltpu.VMEM
     return pl.pallas_call(
         functools.partial(kernel, group, n_outer, n_inner),
@@ -441,6 +551,8 @@
         in_specs=[hbm] * 6 + [pl.BlockSpec(memory_space=pltpu.SMEM)],
         out_specs=(hbm, hbm, hbm),
         scratch_shapes=[
+            vmem(keys.shape, BF16),
+            vmem(values.shape, BF16),
             vmem(wide, BF16),
             vmem(wide, BF16),
             vmem(log_sum.shape, F32),
@@ -448,30 +560,31 @@
             vmem((chunks, group, rows), F32),
             vmem((chunks, group, rows), F32),
             vmem(pair, BF16),
-            vmem(pair, BF16),
-            vmem(pair, BF16),
-            vmem(pair, BF16),
+            vmem((2,) + pair, BF16),
+            vmem(pair, BF16),
+            vmem(pair, BF16),
+            vmem(wide, F32),
             vmem(wide, F32),
             vmem(wide, BF16),
             vmem(pair, F32),
-            vmem(pair, F32),
-            vmem(pair, F32),
-            vmem(pair, BF16),
-            vmem(pair, BF16),
-            vmem(pair, BF16),
-            vmem(pair, BF16),
-            vmem(pair, BF16),
-            vmem(pair, BF16),
-            vmem((4, 8, 128), F32),
+            vmem(pair, BF16),
+            vmem(pair, BF16),
+            vmem(pair, BF16),
+            vmem(pair, BF16),
+            vmem(pair, BF16),
+            vmem(pair, BF16),
+            vmem(pair, BF16),
+            vmem(pair, BF16),
+            vmem((5, 8, 128), F32),
             pltpu.SMEM((4,), jnp.int32),
             pltpu.SemaphoreType.DMA((5, chunks)),
             pltpu.SemaphoreType.DMA((3, chunks)),
-            pltpu.SemaphoreType.DMA((2, 3)),
-            pltpu.SemaphoreType.DMA((6, chunks)),
-            pltpu.SemaphoreType.DMA((6, chunks)),
+            pltpu.SemaphoreType.DMA((2, 4)),
+            pltpu.SemaphoreType.DMA((8, chunks)),
+            pltpu.SemaphoreType.DMA((8, chunks)),
         ],
         compiler_params=pltpu.CompilerParams(
-            collective_id=0 if COMM else None, has_side_effects=True, vmem_limit_bytes=48 * 1024 * 1024
+            collective_id=0 if COMM else None, has_side_effects=True, vmem_limit_bytes=56 * 1024 * 1024
         ),
         cost_estimate=pl.CostEstimate(
             flops=6_000_000_000, bytes_accessed=10_000_000, transcendentals=5_000_000

time: 97.6 us -> 81.6 us (0.84)
  the two profiles are of different devices: /device:TPU:26 before, /device:TPU:22 now
where the time goes in v1:
time: 81.6 us; the launch traced here: 81.5 us
  Pallas kernels  75 us (92%)
  local copies, waits for them, and re-layouts  5.79 us (7%)
    pallas_call x1, Pallas kernels, on_device(): pl.pallas_call(functools.partial(kernel, group, n_outer, n_inner), out_sh...  75 us
    unnamed x7, local copies, waits for them, and re-layouts  5.79 us

profile of v1, /device:TPU:22, one launch (start us, length us, event | category | flops | bytes accessed | tf_op | source)
XLA Modules:
  0.0 81.5 jit_solution(7509549273565715779)
XLA Ops:
  0.6 75.0 %shard_map.94 = (bf16[256,4096]{1,0:T(8,128)(2,1)}, f32[256,1024]{1,0:T(8,128)}, f32[256,1024]{1,0:T(8,128)}) custom-call(bf16[256,4096]{1,0:T(8,128)(2,1)} %q_hbm.1, bf16[256,1024]{1,0:T(8,128)(2,1)} %k_hbm.1, bf16[256,1024]{1,0:T(8,128)(2,1)} %v_hbm.1, bf16[256,4096]{1,0:T(8,128)(2,1)} %do_hbm.1, f32[32,256]{1,0:T(8,128)} %lse_hbm.1, f32[32,256]{1,0:T(8,128)} %delta_hbm.1, ...), custom_call_target="tpu_custom_call" | custom-call | flops 6000000000 | bytes 10000000 | tf_op jit(solution)/shard_map/pallas_call | solution.py:544
  75.7 0.0 copy-start.1
  75.7 3.2 %copy.13 = bf16[256,4096]{1,0:T(8,128)(2,1)} copy(bf16[256,4096]{1,0:T(8,128)(2,1)} %get-tuple-element.6) | data formatting | bytes 4194304
  78.9 0.0 copy-done.1
  78.9 0.0 copy-start
  78.9 1.0 %copy.14 = f32[256,1024]{1,0:T(8,128)} copy(f32[256,1024]{1,0:T(8,128)S(1)} %copy-done.1) | data formatting | bytes 2097152
  79.9 0.6 copy-done
  80.5 1.0 %copy.15 = f32[256,1024]{1,0:T(8,128)} copy(f32[256,1024]{1,0:T(8,128)S(1)} %copy-done) | data formatting | bytes 2097152
Async XLA Ops:
  75.7 3.2 %copy-start.1 = (f32[256,1024]{1,0:T(8,128)S(1)}, f32[256,1024]{1,0:T(8,128)}, u32[]{:S(2)}) copy-start(f32[256,1024]{1,0:T(8,128)} %get-tuple-element.7) | copy-start | bytes 3145732
  78.9 1.6 %copy-start = (f32[256,1024]{1,0:T(8,128)S(1)}, f32[256,1024]{1,0:T(8,128)}, u32[]{:S(2)}) copy-start(f32[256,1024]{1,0:T(8,128)} %get-tuple-element.8) | copy-start | bytes 3145732

commit v2 on v1

--- a/solution.py
+++ b/solution.py
@@ -108,11 +108,11 @@
             device_id_type=MESH,
         )
 
-    def hop_pair(g):
-        return remote(kv_own.at[g], kv_hop.at[odd, g], 0, g, to_pair)
-
-    def hop_far(g):
-        return remote(kv_hop.at[1 - odd, g], kv_far.at[g], 1, g, to_far)
+    def hop_pair(g, x):
+        return remote(kv_own.at[g, x], kv_hop.at[odd, g, x], 8 * x, g, to_pair)
+
+    def hop_far(g, x):
+        return remote(kv_hop.at[1 - odd, g, x], kv_far.at[g, x], 1 + 8 * x, g, to_far)
 
     def hop_up(g):
         return remote(kv_hop.at[1, g], kv_hop.at[0, g], 6, g, to_up)
@@ -220,7 +220,8 @@
 
     def send_own(g, carry):
         if COMM:
-            hop_pair(g).start()
+            for x in range(2):
+                hop_pair(g, x).start()
 
             @pl.when(core == 0)
             def _():
@@ -355,8 +356,9 @@
         def _():
             g = t
             if COMM:
-                hop_pair(g).wait_recv()
-                hop_far(g).start()
+                for x in range(2):
+                    hop_pair(g, x).wait_recv()
+                    hop_far(g, x).start()
 
             @pl.when(g + LEAD < chunks)
             def _():
@@ -391,7 +393,8 @@
         def _():
             g = t - 2
             if COMM:
-                hop_far(g).wait_recv()
+                for x in range(2):
+                    hop_far(g, x).wait_recv()
 
                 @pl.when(core == 1)
                 def _():
@@ -508,8 +511,9 @@
         for copy in store_kv(g):
             copy.wait()
         if COMM:
-            hop_pair(g).wait_send()
-            hop_far(g).wait_send()
+            for x in range(2):
+                hop_pair(g, x).wait_send()
+                hop_far(g, x).wait_send()
             hop_near_own(g).wait_send()
             back_near(g).wait_send()
             back_far(g).wait_send()
@@ -580,8 +584,8 @@
             pltpu.SemaphoreType.DMA((5, chunks)),
             pltpu.SemaphoreType.DMA((3, chunks)),
             pltpu.SemaphoreType.DMA((2, 4)),
-            pltpu.SemaphoreType.DMA((8, chunks)),
-            pltpu.SemaphoreType.DMA((8, chunks)),
+            pltpu.SemaphoreType.DMA((10, chunks)),
+            pltpu.SemaphoreType.DMA((10, chunks)),
         ],
         compiler_params=pltpu.CompilerParams(
             collective_id=0 if COMM else None, has_side_effects=True, vmem_limit_bytes=56 * 1024 * 1024

time: 81.6 us -> 86.2 us (1.056)
  Pallas kernels: 75 us -> 79.6 us
    pallas_call x1, Pallas kernels: 75 us -> 79.6 us  [on_device(): pl.pallas_call(functools.partial(kernel, group, n_outer, n_inner), out_sh...]
where the time goes in v2:
time: 86.2 us; the launch traced here: 86 us
  Pallas kernels  79.6 us (92%)
  local copies, waits for them, and re-layouts  5.79 us (7%)
    pallas_call x1, Pallas kernels, on_device(): pl.pallas_call(functools.partial(kernel, group, n_outer, n_inner), out_sh...  79.6 us
    unnamed x7, local copies, waits for them, and re-layouts  5.79 us

profile of v2, /device:TPU:22, one launch (start us, length us, event | category | flops | bytes accessed | tf_op | source)
XLA Modules:
  0.0 86.0 jit_solution(4803695711305637502)
XLA Ops:
  0.6 79.6 %shard_map.94 = (bf16[256,4096]{1,0:T(8,128)(2,1)}, f32[256,1024]{1,0:T(8,128)}, f32[256,1024]{1,0:T(8,128)}) custom-call(bf16[256,4096]{1,0:T(8,128)(2,1)} %q_hbm.1, bf16[256,1024]{1,0:T(8,128)(2,1)} %k_hbm.1, bf16[256,1024]{1,0:T(8,128)(2,1)} %v_hbm.1, bf16[256,4096]{1,0:T(8,128)(2,1)} %do_hbm.1, f32[32,256]{1,0:T(8,128)} %lse_hbm.1, f32[32,256]{1,0:T(8,128)} %delta_hbm.1, ...), custom_call_target="tpu_custom_call" | custom-call | flops 6000000000 | bytes 10000000 | tf_op jit(solution)/shard_map/pallas_call | solution.py:548
  80.2 0.0 copy-start.1
  80.2 3.2 %copy.13 = bf16[256,4096]{1,0:T(8,128)(2,1)} copy(bf16[256,4096]{1,0:T(8,128)(2,1)} %get-tuple-element.6) | data formatting | bytes 4194304
  83.4 0.0 copy-done.1
  83.4 0.0 copy-start
  83.4 1.0 %copy.14 = f32[256,1024]{1,0:T(8,128)} copy(f32[256,1024]{1,0:T(8,128)S(1)} %copy-done.1) | data formatting | bytes 2097152
  84.4 0.6 copy-done
  85.0 1.0 %copy.15 = f32[256,1024]{1,0:T(8,128)} copy(f32[256,1024]{1,0:T(8,128)S(1)} %copy-done) | data formatting | bytes 2097152
Async XLA Ops:
  80.2 3.2 %copy-start.1 = (f32[256,1024]{1,0:T(8,128)S(1)}, f32[256,1024]{1,0:T(8,128)}, u32[]{:S(2)}) copy-start(f32[256,1024]{1,0:T(8,128)} %get-tuple-element.7) | copy-start | bytes 3145732
  83.4 1.6 %copy-start = (f32[256,1024]{1,0:T(8,128)S(1)}, f32[256,1024]{1,0:T(8,128)}, u32[]{:S(2)}) copy-start(f32[256,1024]{1,0:T(8,128)} %get-tuple-element.8) | copy-start | bytes 3145732
